TPU v7x, 128 devices: a whole 4x4x4 slice. The times are simulated.
128 devices in a mesh: rep: 16 (over z, x_hi, core), sec: 2 (over x_lo), mdl: 4 (over y).
Axes of the slice: x: 4 (x_hi: 2, x_lo: 2; x = x_hi * 2 + x_lo), y: 4, z: 4, core: 2. Of those that a mesh axis runs over, the one named last changes fastest.
Arguments:
- obs: bfloat16 [2, 8192, 1536], P('sec', 'rep'), may hold values from -6 to 6
- a_query: bfloat16 [1536, 1536], P(None, 'mdl'), may hold values from -0.15309311 to 0.15309311
- a_keyval: bfloat16 [2, 1536, 512], P(None, None, 'mdl'), may hold values from -0.15309311 to 0.15309311
- a_out: bfloat16 [1536, 1536], P('mdl'), may hold values from -0.15625 to 0.15625
- w_policy: bfloat16 [1536, 128], replicated, may hold values from -0.15625 to 0.15625
- c_in: bfloat16 [1536, 2048], P(None, 'mdl'), may hold values from -0.15309311 to 0.15309311
- c_query: bfloat16 [2048, 2048], P(None, 'mdl'), may hold values from -0.13258252 to 0.13258252
- c_keyval: bfloat16 [2, 2048, 512], P(None, None, 'mdl'), may hold values from -0.13258252 to 0.13258252
- c_out: bfloat16 [2048, 2048], P('mdl'), may hold values from -0.125 to 0.125
- w_value: bfloat16 [2048], replicated, may hold values from -0.110485435 to 0.110485435
- actions: int32 [2, 8192], P('sec', 'rep'), may hold values from 0 to 127
- advantages: float32 [2, 8192], P('sec', 'rep'), may hold values from -6 to 6
- old_logp: float32 [2, 8192], P('sec', 'rep'), may hold values from -7 to -4
- returns: float32 [2, 8192], P('sec', 'rep'), may hold values from -6 to 6
- robot_count: int32 [2], replicated, may hold values from 2048 to 8192, as said below
Outputs:
- values: float32 [2, 8192], P('sec', ('rep', 'mdl'))
- grad_a_out: float32 [1536, 1536], P('mdl')
- grad_c_out: float32 [2048, 2048], P('mdl')
Inputs may be any that keep to these rules, and one draw needn't show every extreme that they name: `robot_count`: one of the two micro-batches holds all 8192 robots, the other at least 2048; live robots are the first ones.
All inputs are finite; a program needn't handle non-finite values.
Results may differ from a plain program's by a relative error of at most 0.023.
Values may be sent and summed in bfloat16 or wider, within the bound.
A program may use at most 128 MiB of HBM per device.

v0:
```python
import math
import jax
import jax.numpy as jnp
from jax import lax
from jax.sharding import PartitionSpec as P

HEAD = 128
epsilon = 1e-05
clip_range = 0.2
masked_score = -1e30


def rms_normed(values_in):
    return values_in * lax.rsqrt(jnp.mean(values_in * values_in, axis=-1, keepdims=True) + epsilon)


def norm_backward(source, normed, grad_in):
    factor = lax.rsqrt(jnp.mean(source * source, axis=-1, keepdims=True) + epsilon)
    return factor * (grad_in - normed * jnp.mean(grad_in * normed, axis=-1, keepdims=True))


def project(source, w_query, w_keyval):
    normed = rms_normed(source).astype(jnp.bfloat16)
    queries = (
        jnp.dot(normed, w_query, preferred_element_type=jnp.float32) * HEAD ** (-0.5)
    ).astype(jnp.bfloat16)
    keyval = jnp.einsum("rd,cdk->crk", normed, w_keyval, preferred_element_type=jnp.float32).astype(
        jnp.bfloat16
    )
    return (queries, keyval)


def policy_backward(hidden, action_ids, advantage, old_values, live_mask, live_total, w_policy):
    source = hidden.astype(jnp.float32)
    normed = rms_normed(source)
    logits = jnp.dot(normed.astype(jnp.bfloat16), w_policy, preferred_element_type=jnp.float32)
    log_probs = jax.nn.log_softmax(logits, axis=-1)
    onehot = (action_ids[:, None] == lax.broadcasted_iota(jnp.int32, logits.shape, 1)).astype(
        jnp.float32
    )
    chosen = jnp.sum(onehot * log_probs, axis=-1)
    prob_ratio = jnp.exp(chosen - old_values)
    plain_term = prob_ratio * advantage
    bounded = jnp.clip(prob_ratio, 1.0 - clip_range, 1.0 + clip_range) * advantage
    slope_term = jnp.where(
        live_mask & (plain_term <= bounded), -plain_term / live_total, jnp.float32(0.0)
    )
    dlogits = slope_term[:, None] * (onehot - jnp.exp(log_probs))
    dnormed = jnp.dot(dlogits, w_policy.astype(jnp.float32).T, precision=lax.Precision.HIGHEST)
    return norm_backward(source, normed, dnormed)


def value_backward(mixed_out, target, live_mask, live_total, w_value):
    normed = rms_normed(mixed_out)
    value_pred = jnp.dot(normed.astype(jnp.bfloat16), w_value, preferred_element_type=jnp.float32)
    slope_term = jnp.where(live_mask, value_pred - target, jnp.float32(0.0)) / live_total
    dnormed = slope_term[:, None] * w_value.astype(jnp.float32)[None, :]
    return (value_pred, norm_backward(mixed_out, normed, dnormed))


def split_heads(queries, kv_heads):
    row_count = queries.shape[0]
    groups = queries.shape[1] // HEAD // kv_heads
    return queries.reshape(row_count, kv_heads, groups, HEAD)


def start_state(heads_in):
    row_count, kv_heads, groups, _ = heads_in.shape
    row_top = jnp.full((kv_heads, groups, row_count), masked_score, jnp.float32)
    row_sum = jnp.zeros((kv_heads, groups, row_count), jnp.float32)
    acc_sum = jnp.zeros((kv_heads, groups, row_count, HEAD), jnp.float32)
    return (row_top, row_sum, acc_sum)


def make_fold(heads_in, robot_total, carried, piece):
    kv_heads = heads_in.shape[1]
    piece_rows = piece.shape[1]
    block_rows = math.gcd(piece_rows, 512)
    block_count = piece_rows // block_rows
    key_blocks = piece[0].reshape(block_count, block_rows, kv_heads, HEAD)
    value_blocks = piece[1].reshape(block_count, block_rows, kv_heads, HEAD)

    def absorb(inner, block_item):
        block_index, key_block, value_block = block_item
        first_key = block_index * block_rows
        row_top, row_sum, acc_sum = inner
        scores = jnp.einsum(
            "rkgd,jkd->kgrj", heads_in, key_block, preferred_element_type=jnp.float32
        )
        key_live = first_key + lax.iota(jnp.int32, block_rows) < robot_total
        scores = jnp.where(key_live, scores, masked_score)
        new_top = jnp.maximum(row_top, jnp.max(scores, axis=-1))
        rescale = jnp.exp(row_top - new_top)
        weights = jnp.exp(scores - new_top[..., None])
        row_sum = row_sum * rescale + jnp.sum(weights, axis=-1)
        value_float = value_block.astype(jnp.float32)
        acc_sum = acc_sum * rescale[..., None] + jnp.einsum(
            "kgrj,jkd->kgrd", weights, value_float, precision=lax.Precision.HIGHEST
        )
        return ((new_top, row_sum, acc_sum), None)

    result, _ = lax.scan(
        absorb, carried, (jnp.arange(block_count, dtype=jnp.int32), key_blocks, value_blocks)
    )
    return result


def finish_heads(carried):
    _, row_sum, acc_sum = carried
    combined = acc_sum / row_sum[..., None]
    kv_heads, groups, row_count, _ = combined.shape
    return (
        jnp.transpose(combined, (2, 0, 1, 3))
        .reshape(row_count, kv_heads * groups * HEAD)
        .astype(jnp.bfloat16)
    )


def on_device(
    obs,
    a_query,
    a_keyval,
    a_out,
    w_policy,
    c_in,
    c_query,
    c_keyval,
    c_out,
    w_value,
    actions,
    advantages,
    old_logp,
    returns,
    robot_count,
):
    row_count = obs.shape[1]
    batch_index = lax.axis_index("sec")
    robot_total = robot_count[batch_index]
    live_total = jnp.sum(robot_count).astype(jnp.float32)
    first_row = lax.axis_index("rep") * row_count
    live_mask = first_row + lax.iota(jnp.int32, row_count) < robot_total
    mdl_count = lax.axis_size("mdl")
    part_rows = row_count // mdl_count
    row_start = lax.axis_index("mdl") * part_rows
    obs_float = obs[0].astype(jnp.float32)
    queries, keyval = project(obs_float, a_query, a_keyval)
    heads_a = split_heads(queries, keyval.shape[2] // HEAD)
    state_a = make_fold(
        heads_a,
        robot_total,
        start_state(heads_a),
        lax.all_gather(keyval, "rep", axis=1, tiled=True),
    )
    attended = finish_heads(state_a)
    mixed_sum = lax.psum(jnp.dot(attended, a_out, preferred_element_type=jnp.float32), "mdl")
    hidden = (obs_float + mixed_sum).astype(jnp.bfloat16)
    dhidden = policy_backward(
        hidden, actions[0], advantages[0], old_logp[0], live_mask, live_total, w_policy
    ).astype(jnp.bfloat16)
    actor_grad = jnp.einsum("rh,rd->hd", attended, dhidden, preferred_element_type=jnp.float32)
    embed_part = jnp.dot(hidden, c_in, preferred_element_type=jnp.float32).astype(jnp.bfloat16)
    embedded = lax.all_gather(embed_part, "mdl", axis=1, tiled=True)
    embed_float = embedded.astype(jnp.float32)
    critic_queries, critic_keyval = project(embed_float, c_query, c_keyval)
    heads_c = split_heads(critic_queries, critic_keyval.shape[2] // HEAD)
    state_c = make_fold(
        heads_c,
        robot_total,
        start_state(heads_c),
        lax.all_gather(critic_keyval, "rep", axis=1, tiled=True),
    )
    critic_attended = finish_heads(state_c)
    critic_sum = lax.psum(
        jnp.dot(critic_attended, c_out, preferred_element_type=jnp.float32).astype(jnp.bfloat16),
        "mdl",
    ).astype(jnp.float32)
    value_pred, dmixed = value_backward(
        embed_float + critic_sum, returns[0], live_mask, live_total, w_value
    )
    value_part = lax.dynamic_slice_in_dim(value_pred, row_start, part_rows, 0)
    dmixed_all = dmixed.astype(jnp.bfloat16)
    critic_grad = jnp.einsum(
        "rh,rd->hd", critic_attended, dmixed_all, preferred_element_type=jnp.float32
    )
    actor_summed, critic_summed = (
        lax.psum(actor_grad.astype(jnp.bfloat16), ("rep", "sec")).astype(jnp.float32),
        lax.psum(critic_grad.astype(jnp.bfloat16), ("rep", "sec")).astype(jnp.float32),
    )
    return (value_part[None, :], actor_summed, critic_summed)


def solution(mesh):
    return jax.shard_map(
        on_device,
        mesh=mesh,
        in_specs=(
            P("sec", "rep", None),
            P(None, "mdl"),
            P(None, None, "mdl"),
            P("mdl", None),
            P(),
            P(None, "mdl"),
            P(None, "mdl"),
            P(None, None, "mdl"),
            P("mdl", None),
            P(),
            P("sec", "rep"),
            P("sec", "rep"),
            P("sec", "rep"),
            P("sec", "rep"),
            P(),
        ),
        out_specs=(P("sec", ("rep", "mdl")), P("mdl", None), P("mdl", None)),
        check_vma=False,
    )
```

profile of v0, /device:TPU:1, one launch (start us, length us, event | category | flops | bytes accessed | tf_op | source)
XLA Modules:
  0.0 878.9 jit_solution(12537995733930431458)
XLA Ops:
  17.4 53.9 %all-gather.4.cloned.1.call-done = bf16[2,8192,128]{2,1,0:T(8,128)(2,1)} async-done(((bf16[2,512,128]{2,1,0:T(8,128)(2,1)}), bf16[2,8192,128]{2,1,0:T(8,128)(2,1)}) %all-gather.4.cloned.1.call-update) | async-done | bytes 4194320 | tf_op jit(solution)/shard_map/all_gather | solution.py:152
  71.4 4.5 fusion.116
  75.9 188.8 %while.30 = (s32[]{:T(128)}, f32[1,3,512]{2,1,0:T(4,128)S(1)}, f32[1,3,512]{2,1,0:T(4,128)S(1)}, f32[1,3,512,128]{3,2,1,0:T(8,128)S(1)}, s32[16]{0:T(128)S(1)}, ...) while((s32[]{:T(128)}, f32[1,3,512]{2,1,0:T(4,128)S(1)}, ...), condition=%wide.region_4.5_spmd.clone, body=%wide.region_1.4_spmd.clone.sunk | while | flops 1415391232 | bytes 24348876 | solution.py:102
  95.5 3.9 fusion.148
  107.3 3.9 fusion.148
  119.1 3.9 fusion.148
  130.9 3.9 fusion.148
  267.0 3.9 fusion.118
  271.0 73.2 %all-reduce.5.cloned.1.call-done = f32[512,1536]{1,0:T(8,128)} async-done(((f32[512,1536]{1,0:T(8,128)}), f32[512,1536]{1,0:T(8,128)}) %all-reduce.5.cloned.1.call-update) | async-done | bytes 3145744 | tf_op jit(solution)/shard_map/psum | solution.py:155
  350.9 30.8 %all-gather.6.cloned.1.call-done = bf16[512,2048]{1,0:T(8,128)(2,1)} async-done(((bf16[512,512]{1,0:T(8,128)(2,1)}), bf16[512,2048]{1,0:T(8,128)(2,1)}) %all-gather.6.cloned.1.call-update) | async-done | bytes 2097168 | tf_op jit(solution)/shard_map/all_gather | solution.py:162
  387.1 4.4 fusion.84
  393.5 49.4 %all-gather.8.cloned.1.call-done = bf16[2,8192,128]{2,1,0:T(8,128)(2,1)} async-done(((bf16[2,512,128]{2,1,0:T(8,128)(2,1)}), bf16[2,8192,128]{2,1,0:T(8,128)(2,1)}) %all-gather.8.cloned.1.call-update) | async-done | bytes 4194320 | tf_op jit(solution)/shard_map/all_gather | solution.py:170
  442.8 4.5 fusion.115
  447.4 234.7 %while.31 = (s32[]{:T(128)}, f32[1,4,512]{2,1,0:T(4,128)S(1)}, f32[1,4,512]{2,1,0:T(4,128)}, f32[1,4,512,128]{3,2,1,0:T(8,128)S(1)}, s32[16]{0:T(128)S(1)}, /*in...) while((s32[]{:T(128)}, f32[1,4,512]{2,1,0:T(4,128)S(1)}, ...), condition=%wide.region_10.11_spmd.clone, body=%wide.region_7.10_spmd.clone.sunk | while | flops 1887187968 | bytes 32447348 | solution.py:102
  457.1 4.9 fusion.153
  471.7 4.9 fusion.153
  486.4 4.9 fusion.153
  501.1 4.9 fusion.153
  515.7 4.9 fusion.153
  530.4 4.9 fusion.153
  545.1 4.9 fusion.153
  559.7 4.9 fusion.153
  574.4 4.9 fusion.153
  589.1 4.9 fusion.153
  603.8 4.9 fusion.153
  618.4 4.9 fusion.153
  633.1 4.9 fusion.153
  647.8 4.9 fusion.153
  662.4 4.9 fusion.153
  677.1 4.9 fusion.153
  691.4 52.2 %all-reduce.7.cloned.1.call-done = bf16[512,2048]{1,0:T(8,128)(2,1)} async-done(((bf16[512,2048]{1,0:T(8,128)(2,1)}), bf16[512,2048]{1,0:T(8,128)(2,1)}) %all-reduce.7.cloned.1.call-update) | async-done | bytes 2097168 | tf_op jit(solution)/shard_map/psum | solution.py:173
  757.4 109.0 %all-reduce.9.cloned.1.call-done = (bf16[384,1536]{1,0:T(8,128)(2,1)}, bf16[512,2048]{1,0:T(8,128)(2,1)}) async-done(((bf16[384,1536]{1,0:T(8,128)(2,1)}, bf16[512,2048]{1,0:T(8,128)(2,1)}), (bf16[384,1536]{1,0:T(8,128)(2,1)}, bf16[512,2048]{1,0:T(8,128)(2,1)})) %all-reduce.9.cloned.1.call-update) | async-done | bytes 3276816 | tf_op jit(solution)/shard_map/psum | solution.py:186
  (584 shorter events, 359.9 us)
Async XLA Ops:
  7.2 677.6 %copy-start = (bf16[512,2048]{1,0:T(8,128)(2,1)S(1)}, bf16[512,2048]{1,0:T(8,128)(2,1)}, u32[]{:S(2)}) copy-start(bf16[512,2048]{1,0:T(8,128)(2,1)} %param.27) | copy-start | bytes 6291460
  7.2 64.2 %all-gather.4.cloned.1.call-start = ((), (), s32[]{:S(2)}) async-start(), calls=%async_computation | async-start | bytes 4456448 | tf_op jit(solution)/shard_map/all_gather | solution.py:152
  12.1 332.1 %all-reduce.5.cloned.1.call-start = ((), (), s32[]{:S(2)}) async-start(), calls=%async_computation.1 | async-start | bytes 6291456 | tf_op jit(solution)/shard_map/psum | solution.py:155
  271.0 110.7 %all-gather.6.cloned.1.call-start = ((), (), s32[]{:S(2)}) async-start(), calls=%async_computation.2 | async-start | bytes 2621440 | tf_op jit(solution)/shard_map/all_gather | solution.py:162
  349.0 34.7 %copy-start.20 = (bf16[2,2048,128]{2,1,0:T(8,128)(2,1)S(1)}, bf16[2,2048,128]{2,1,0:T(8,128)(2,1)}, u32[]{:S(2)}) copy-start(bf16[2,2048,128]{2,1,0:T(8,128)(2,1)} %param.26) | copy-start | bytes 3145732
  350.8 92.0 %all-gather.8.cloned.1.call-start = ((), (), s32[]{:S(2)}) async-start(), calls=%async_computation.3 | async-start | bytes 4456448 | tf_op jit(solution)/shard_map/all_gather | solution.py:170
  386.8 356.8 %all-reduce.7.cloned.1.call-start = ((), (), s32[]{:S(2)}) async-start(), calls=%async_computation.4 | async-start | bytes 4194304 | tf_op jit(solution)/shard_map/psum | solution.py:173
  456.8 5.2 copy-start.10
  457.1 5.0 copy-start.24
  471.4 5.2 copy-start.10
  486.1 5.2 copy-start.10
  486.4 5.0 copy-start.24
  500.8 5.2 copy-start.10
  501.1 5.0 copy-start.24
  515.5 5.2 copy-start.10
  515.7 5.0 copy-start.24
  530.1 5.2 copy-start.10
  544.8 5.2 copy-start.10
  545.1 5.0 copy-start.24
  559.5 5.2 copy-start.10
  559.7 5.0 copy-start.24
  574.1 5.2 copy-start.10
  574.4 5.0 copy-start.24
  588.8 5.2 copy-start.10
  603.5 5.2 copy-start.10
  618.1 5.2 copy-start.10
  632.8 5.2 copy-start.10
  647.5 5.2 copy-start.10
  662.2 5.2 copy-start.10
  662.4 5.0 copy-start.24
  676.8 5.2 copy-start.10
  687.4 179.0 %all-reduce.9.cloned.1.call-start = ((), (), s32[]{:S(2)}) async-start(), calls=%async_computation.5 | async-start | bytes 6553600 | tf_op jit(solution)/shard_map/psum | solution.py:186
  (119 other events, 327.2 us)
Sparse Core Ops, SparseCore 0:
  12.2 59.0 all-gather.3
  271.1 73.0 all-reduce.4
  350.9 30.6 all-gather.5
  386.9 55.8 all-gather.7
  687.5 56.0 all-reduce.6
  756.9 109.4 all-reduce.8
where the time goes:
time: 881 us; the launch traced here: 879 us
  waiting for transfers between devices  369 us (42%)
  matrix products  286 us (32%)
  other arithmetic  135 us (15%)
  local copies, waits for them, and re-layouts  50.4 us (6%)
  loops' own time  23.5 us (3%)
  between operations  15.1 us (2%)
    dot_general x32, matrix products, absorb(): jnp.einsum('kgrj,jkd->kgrd', weights, value_float, precision=lax.Precisio...  142 us
    dot_general x32, matrix products, absorb(): jnp.einsum('rkgd,jkd->kgrj', heads_in, key_block, preferred_element_type=...  112 us
    psum x1, waiting for transfers between devices, on_device(): lax.psum(actor_grad.astype(jnp.bfloat16), ('rep', 'sec'))  109 us
    reduce_sum x32, other arithmetic, absorb(): row_sum = row_sum * rescale + jnp.sum(weights, axis=-1)  92.6 us
    psum x1, waiting for transfers between devices, on_device(): lax.psum(jnp.dot(attended, a_out, preferred_element_type=jnp.float32), 'm...  73.2 us
    all_gather x1, waiting for transfers between devices, on_device(): lax.all_gather(keyval, 'rep', axis=1, tiled=True)  53.9 us
    psum x1, waiting for transfers between devices, on_device(): lax.psum(jnp.dot(critic_attended, c_out, preferred_element_type=jnp.float...  52.2 us
    all_gather x1, waiting for transfers between devices, on_device(): lax.all_gather(critic_keyval, 'rep', axis=1, tiled=True)  49.4 us
  transfers between devices with their start and end apart: 6, of which 6 were waited for; matrix products, arithmetic and copies ran while one was open for 2% of the time, Pallas kernels for 0%

commit v1 on v0

--- a/solution.py
+++ b/solution.py
@@ -3,6 +3,7 @@
 import jax.numpy as jnp
 from jax import lax
 from jax.sharding import PartitionSpec as P
+from jax.lax import psum
 
 HEAD = 128
 epsilon = 1e-05
@@ -133,6 +134,11 @@
     returns,
     robot_count,
 ):
+
+    def _try_all_seats_all(raw):
+        p_next = psum(raw, "rep")
+        return psum(p_next, "sec")
+
     row_count = obs.shape[1]
     batch_index = lax.axis_index("sec")
     robot_total = robot_count[batch_index]
@@ -183,7 +189,7 @@
         "rh,rd->hd", critic_attended, dmixed_all, preferred_element_type=jnp.float32
     )
     actor_summed, critic_summed = (
-        lax.psum(actor_grad.astype(jnp.bfloat16), ("rep", "sec")).astype(jnp.float32),
+        _try_all_seats_all(actor_grad.astype(jnp.bfloat16)).astype(jnp.float32),
         lax.psum(critic_grad.astype(jnp.bfloat16), ("rep", "sec")).astype(jnp.float32),
     )
     return (value_part[None, :], actor_summed, critic_summed)

time: 881 us -> 876 us (level)
  other arithmetic: 135 us -> 69.1 us
  matrix products: 286 us -> 327 us
  waiting for transfers between devices: 369 us -> 403 us
  local copies, waits for them, and re-layouts: 50.4 us -> 37.1 us
    reduce_sum x32, other arithmetic: 92.6 us -> 22.1 us  [absorb(): row_sum = row_sum * rescale + jnp.sum(weights, axis=-1)]
    psum x1 -> x3, waiting for transfers between devices: 109 us -> 152 us  [the longest x1 109 us: on_device(): lax.psum(critic_grad.astype(jnp.bfloat16), ('rep', 'sec'))]
    dot_general x32, matrix products: 142 us -> 182 us  [absorb(): jnp.einsum('kgrj,jkd->kgrd', weights, value_float, precision=lax.Precisio...]
    while x288 -> x96, local copies, waits for them, and re-layouts: 14.1 us -> 0.25 us
    all_gather x1, waiting for transfers between devices: 49.4 us -> 37.3 us  [on_device(): lax.all_gather(critic_keyval, 'rep', axis=1, tiled=True)]
  transfers between devices with their start and end apart: 6 -> 8, of which waited for: 6 -> 7; matrix products, arithmetic and copies ran while one was open for 2% -> 27% of each run, Pallas kernels for 0% -> 0%
where the time goes in v1:
time: 876 us; the launch traced here: 874 us
  waiting for transfers between devices  403 us (46%)
  matrix products  327 us (37%)
  other arithmetic  69.1 us (8%)
  local copies, waits for them, and re-layouts  37.1 us (4%)
  loops' own time  22.7 us (3%)
  between operations  15 us (2%)
    dot_general x32, matrix products, absorb(): jnp.einsum('kgrj,jkd->kgrd', weights, value_float, precision=lax.Precisio...  182 us
    dot_general x32, matrix products, absorb(): jnp.einsum('rkgd,jkd->kgrj', heads_in, key_block, preferred_element_type=...  112 us
    psum x1, waiting for transfers between devices, on_device(): lax.psum(critic_grad.astype(jnp.bfloat16), ('rep', 'sec'))  109 us
    psum x1, waiting for transfers between devices, on_device(): lax.psum(jnp.dot(attended, a_out, preferred_element_type=jnp.float32), 'm...  73.2 us
    psum x1, waiting for transfers between devices, on_device(): lax.psum(jnp.dot(critic_attended, c_out, preferred_element_type=jnp.float...  55.3 us
    all_gather x1, waiting for transfers between devices, on_device(): lax.all_gather(keyval, 'rep', axis=1, tiled=True)  53.9 us
    psum x1, waiting for transfers between devices, _try_all_seats_all(): return psum(p_next, 'sec')  42.8 us
    all_gather x1, waiting for transfers between devices, on_device(): lax.all_gather(critic_keyval, 'rep', axis=1, tiled=True)  37.3 us
  transfers between devices with their start and end apart: 8, of which 7 were waited for; matrix products, arithmetic and copies ran while one was open for 27% of the time, Pallas kernels for 0%

profile of v1, /device:TPU:1, one launch (start us, length us, event | category | flops | bytes accessed | tf_op | source)
XLA Modules:
  0.0 874.4 jit_solution(1754287841930516157)
XLA Ops:
  17.5 53.9 %all-gather.4.cloned.1.call-done = bf16[2,8192,128]{2,1,0:T(8,128)(2,1)} async-done(((bf16[2,512,128]{2,1,0:T(8,128)(2,1)}), bf16[2,8192,128]{2,1,0:T(8,128)(2,1)}) %all-gather.4.cloned.1.call-update) | async-done | bytes 4194320 | tf_op jit(solution)/shard_map/all_gather | solution.py:158
  75.9 171.9 %while.30 = (s32[]{:T(128)}, f32[1,3,512]{2,1,0:T(4,128)S(1)}, f32[1,3,512]{2,1,0:T(4,128)S(1)}, f32[1,3,512,128]{3,2,1,0:T(8,128)S(1)}, s32[16]{0:T(128)S(1)}, ...) while((s32[]{:T(128)}, f32[1,3,512]{2,1,0:T(4,128)S(1)}, ...), condition=%wide.region_4.5_spmd.clone, body=%wide.region_1.4_spmd.clone.sunk | while | flops 1415391232 | bytes 24349884 | solution.py:103
  80.9 5.0 fusion.148
  91.6 5.0 fusion.148
  102.4 5.0 fusion.148
  113.1 5.0 fusion.148
  123.9 5.0 fusion.148
  166.9 5.0 fusion.148
  209.8 5.0 fusion.148
  254.2 73.2 %all-reduce.6.cloned.1.call-done = f32[512,1536]{1,0:T(8,128)} async-done(((f32[512,1536]{1,0:T(8,128)}), f32[512,1536]{1,0:T(8,128)}) %all-reduce.6.cloned.1.call-update) | async-done | bytes 3145744 | tf_op jit(solution)/shard_map/psum | solution.py:161
  334.0 30.8 %all-gather.6.cloned.1.call-done = bf16[512,2048]{1,0:T(8,128)(2,1)} async-done(((bf16[512,512]{1,0:T(8,128)(2,1)}), bf16[512,2048]{1,0:T(8,128)(2,1)}) %all-gather.6.cloned.1.call-update) | async-done | bytes 2097168 | tf_op jit(solution)/shard_map/all_gather | solution.py:168
  389.3 37.3 %all-gather.8.cloned.1.call-done = bf16[2,8192,128]{2,1,0:T(8,128)(2,1)} async-done(((bf16[2,512,128]{2,1,0:T(8,128)(2,1)}), bf16[2,8192,128]{2,1,0:T(8,128)(2,1)}) %all-gather.8.cloned.1.call-update) | async-done | bytes 4194320 | tf_op jit(solution)/shard_map/all_gather | solution.py:176
  431.1 206.6 %while.31 = (s32[]{:T(128)}, f32[1,4,512]{2,1,0:T(4,128)S(1)}, f32[1,4,512]{2,1,0:T(4,128)S(1)}, f32[1,4,512,128]{3,2,1,0:T(8,128)S(1)}, s32[16]{0:T(128)S(1)}, ...) while((s32[]{:T(128)}, f32[1,4,512]{2,1,0:T(4,128)S(1)}, ...), condition=%wide.region_10.11_spmd.clone, body=%wide.region_7.10_spmd.clone.sunk | while | flops 1887187968 | bytes 32378044 | solution.py:103
  436.8 6.3 fusion.153
  449.7 6.3 fusion.153
  462.6 6.3 fusion.153
  475.5 6.4 fusion.153
  488.5 6.3 fusion.153
  501.4 6.3 fusion.153
  514.3 6.3 fusion.153
  527.2 6.3 fusion.153
  540.1 6.3 fusion.153
  553.0 6.3 fusion.153
  565.9 6.3 fusion.153
  578.8 6.3 fusion.153
  591.8 6.3 fusion.153
  604.7 6.3 fusion.153
  617.6 6.3 fusion.153
  630.5 6.3 fusion.153
  644.0 55.3 %all-reduce.8.cloned.1.call-done = bf16[512,2048]{1,0:T(8,128)(2,1)} async-done(((bf16[512,2048]{1,0:T(8,128)(2,1)}), bf16[512,2048]{1,0:T(8,128)(2,1)}) %all-reduce.8.cloned.1.call-update) | async-done | bytes 2097168 | tf_op jit(solution)/shard_map/psum | solution.py:179
  708.4 42.8 %all-reduce.12.cloned.1.call-done = bf16[384,1536]{1,0:T(8,128)(2,1)} async-done(((bf16[384,1536]{1,0:T(8,128)(2,1)}), bf16[384,1536]{1,0:T(8,128)(2,1)}) %all-reduce.12.cloned.1.call-update) | async-done | bytes 1179664 | tf_op jit(solution)/shard_map/psum | solution.py:140
  754.7 108.8 %all-reduce.14.cloned.1.call-done = bf16[512,2048]{1,0:T(8,128)(2,1)} async-done(((bf16[512,2048]{1,0:T(8,128)(2,1)}), bf16[512,2048]{1,0:T(8,128)(2,1)}) %all-reduce.14.cloned.1.call-update) | async-done | bytes 2097168 | tf_op jit(solution)/shard_map/psum | solution.py:193
  (389 shorter events, 298.1 us)
Async XLA Ops:
  7.2 633.2 %copy-start = (bf16[512,2048]{1,0:T(8,128)(2,1)S(1)}, bf16[512,2048]{1,0:T(8,128)(2,1)}, u32[]{:S(2)}) copy-start(bf16[512,2048]{1,0:T(8,128)(2,1)} %param.27) | copy-start | bytes 6291460
  7.2 64.2 %all-gather.4.cloned.1.call-start = ((), (), s32[]{:S(2)}) async-start(), calls=%async_computation | async-start | bytes 4456448 | tf_op jit(solution)/shard_map/all_gather | solution.py:158
  12.1 315.3 %all-reduce.6.cloned.1.call-start = ((), (), s32[]{:S(2)}) async-start(), calls=%async_computation.1 | async-start | bytes 6291456 | tf_op jit(solution)/shard_map/psum | solution.py:161
  80.9 5.1 copy-start.2
  123.9 5.1 copy-start.2
  166.8 5.1 copy-start.2
  209.8 5.1 copy-start.2
  254.1 110.6 %all-gather.6.cloned.1.call-start = ((), (), s32[]{:S(2)}) async-start(), calls=%async_computation.2 | async-start | bytes 2621440 | tf_op jit(solution)/shard_map/all_gather | solution.py:168
  332.1 35.3 %copy-start.12 = (bf16[2,2048,128]{2,1,0:T(8,128)(2,1)S(1)}, bf16[2,2048,128]{2,1,0:T(8,128)(2,1)}, u32[]{:S(2)}) copy-start(bf16[2,2048,128]{2,1,0:T(8,128)(2,1)} %param.26) | copy-start | bytes 3145732
  333.9 92.6 %all-gather.8.cloned.1.call-start = ((), (), s32[]{:S(2)}) async-start(), calls=%async_computation.3 | async-start | bytes 4456448 | tf_op jit(solution)/shard_map/all_gather | solution.py:176
  370.5 272.6 %all-reduce.10.cloned.1.call-start = ((), (), s32[]{:S(2)}) async-start(), calls=%async_computation.5 | async-start | bytes 2359296 | tf_op jit(solution)/shard_map/psum | solution.py:139
  372.8 5.2 copy-start.5
  372.8 5.2 copy-start.7
  382.8 316.5 %all-reduce.8.cloned.1.call-start = ((), (), s32[]{:S(2)}) async-start(), calls=%async_computation.4 | async-start | bytes 4194304 | tf_op jit(solution)/shard_map/psum | solution.py:179
  436.8 6.4 copy-start.1
  449.7 6.4 copy-start.1
  462.6 6.4 copy-start.1
  475.5 6.4 copy-start.1
  488.5 6.4 copy-start.1
  501.4 6.4 copy-start.1
  514.3 6.4 copy-start.1
  527.2 6.4 copy-start.1
  540.1 6.4 copy-start.1
  553.0 6.4 copy-start.1
  565.9 6.4 copy-start.1
  578.8 6.4 copy-start.1
  591.7 6.4 copy-start.1
  604.7 6.4 copy-start.1
  617.6 6.4 copy-start.1
  630.5 6.4 copy-start.1
  643.0 108.2 %all-reduce.12.cloned.1.call-start = ((), (), s32[]{:S(2)}) async-start(), calls=%async_computation.6 | async-start | bytes 2359296 | tf_op jit(solution)/shard_map/psum | solution.py:140
  643.7 219.7 %all-reduce.14.cloned.1.call-start = ((), (), s32[]{:S(2)}) async-start(), calls=%async_computation.7 | async-start | bytes 4194304 | tf_op jit(solution)/shard_map/psum | solution.py:193
  (20 other events, 82.6 us)
Sparse Core Ops, SparseCore 0:
  12.2 59.0 all-gather.3
  254.2 73.0 all-reduce.5
  334.0 30.6 all-gather.5
  370.6 55.8 all-gather.7
  428.9 138.5 all-reduce.9
  643.1 56.1 all-reduce.7
  701.8 49.2 all-reduce.11
  755.0 108.4 all-reduce.13
